TPU v7x, 256 devices: a whole 4x4x8 slice. The times are simulated.
256 devices in a mesh: dp: 32 (over z_lo, x, core), rows: 8 (over z_hi, y).
Axes of the slice: x: 4, y: 4, z: 8 (z_hi: 2, z_lo: 4; z = z_hi * 4 + z_lo), core: 2. Of those that a mesh axis runs over, the one named last changes fastest.
Arguments:
- features: bfloat16 [64, 48, 64, 1024], P('dp', 'rows'), may hold values from -8 to 8
- first_atrous_weight: bfloat16 [3, 3, 1024, 256], P(None, None, 'dp'), may hold values from -0.0625 to 0.0625
- second_atrous_weight: bfloat16 [3, 3, 1024, 256], P(None, None, 'dp'), may hold values from -0.0625 to 0.0625
- third_atrous_weight: bfloat16 [3, 3, 1024, 256], P(None, None, 'dp'), may hold values from -0.0625 to 0.0625
- pointwise_weight: bfloat16 [1024, 256], replicated, may hold values from -0.1875 to 0.1875
- pooling_weight: bfloat16 [1024, 256], replicated, may hold values from -0.1875 to 0.1875
- projection_weight: bfloat16 [1280, 256], replicated, may hold values from -0.15625 to 0.15625
- branch_norm_gain: float32 [4, 256], replicated, may hold values from 0.25 to 1.75
- branch_norm_shift: float32 [4, 256], replicated, may hold values from -3 to 3
- projection_norm_gain: float32 [256], replicated, may hold values from 0.25 to 1.75
- projection_norm_shift: float32 [256], replicated, may hold values from -3 to 3
- ghost_group_index: int32 [64], replicated, may hold values from 0 to 15, as said below
Outputs:
- decoder_in: bfloat16 [64, 48, 64, 256], P(None, 'rows', 'dp')
Inputs may be any that keep to these rules, and one draw needn't show every extreme that they name: `ghost_group_index`: each of the 16 group ids names exactly 4 images.
All inputs are finite; a program needn't handle non-finite values.
Results may differ from a plain program's by a relative error of at most 0.0014.
The roundings to bfloat16 on the way count: a program that leaves them out, or rounds other values in their place, can miss the bound.
Values may be sent and summed in bfloat16 or wider, within the bound.
A program may use at most 128 MiB of HBM per device.

v0:
```python
import jax
import jax.numpy as jnp
from jax import lax
from jax.sharding import PartitionSpec as P

DILATION_FIRST = 12
DILATION_SECOND = 24
DILATION_THIRD = 36


def from_behind(array, axis, by):
    count = lax.axis_size(axis)
    pairs = [(i, i + by) for i in range(count) if 0 <= i + by < count]
    return lax.ppermute(array, axis, pairs)


def row_tap_list(block_tensor, kernel_row_slice, dilation_rate):
    partial_terms = jnp.einsum(
        "irwc,kco->irwko", block_tensor, kernel_row_slice, preferred_element_type=jnp.float32
    )
    map_width = block_tensor.shape[2]
    left_padding = jnp.pad(partial_terms[:, :, :, 0], ((0, 0), (0, 0), (dilation_rate, 0), (0, 0)))[
        :, :, :map_width
    ]
    right_padding = jnp.pad(
        partial_terms[:, :, :, 2], ((0, 0), (0, 0), (0, dilation_rate), (0, 0))
    )[:, :, dilation_rate:]
    return partial_terms[:, :, :, 1] + left_padding + right_padding


def dilated_result(features, kernel_weight, dilation_rate):
    step_offsets = dilation_rate // features.shape[1]
    running_sum = row_tap_list(features, kernel_weight[1], dilation_rate)
    for by_dev, tap_offset in ((step_offsets, 0), (-step_offsets, 2)):
        shifted_rows = from_behind(features, "rows", by_dev)
        running_sum = running_sum + row_tap_list(
            shifted_rows, kernel_weight[tap_offset], dilation_rate
        )
    return running_sum


def stats_terms(pre, onehot):
    first = jnp.sum(pre, axis=(1, 2))
    second = jnp.sum(pre * pre, axis=(1, 2))
    group_first = jnp.dot(onehot.T, first, precision=lax.Precision.HIGHEST)
    group_second = jnp.dot(onehot.T, second, precision=lax.Precision.HIGHEST)
    return (group_first, group_second)


def apply_norm(pre, onehot, total_first, total_second, count, gain, shift):
    mean = total_first / count
    var = total_second / count - mean * mean
    inv = lax.rsqrt(var + 1e-05)
    img_mean = jnp.dot(onehot, mean, precision=lax.Precision.HIGHEST)
    img_inv = jnp.dot(onehot, inv, precision=lax.Precision.HIGHEST)
    scaled = (pre - img_mean[:, None, None, :]) * img_inv[:, None, None, :] * gain + shift
    return jax.nn.relu(scaled).astype(jnp.bfloat16)


def project(joined, onehot, projection_weight, count, projection_norm_gain, projection_norm_shift):
    proj = jnp.einsum(
        "irwc,co->irwo", joined, projection_weight, preferred_element_type=jnp.float32
    )
    group_first, group_second = stats_terms(proj, onehot)
    total_first, total_second = lax.psum((group_first, group_second), ("dp", "rows"))
    return apply_norm(
        proj, onehot, total_first, total_second, count, projection_norm_gain, projection_norm_shift
    )


def shards(
    features,
    first_atrous_weight,
    second_atrous_weight,
    third_atrous_weight,
    pointwise_weight,
    pooling_weight,
    projection_weight,
    branch_norm_gain,
    branch_norm_shift,
    projection_norm_gain,
    projection_norm_shift,
    ghost_group_index,
):
    img_dev, rows_dev, cols, chans = features.shape
    dp_size = lax.axis_size("dp")
    rows_size = lax.axis_size("rows")
    images = img_dev * dp_size
    groups = images // 4
    pixels = rows_dev * rows_size * cols
    count = 4.0 * pixels
    start = lax.axis_index("dp") * img_dev
    labels = jnp.arange(groups, dtype=jnp.int32)
    all_hot = (ghost_group_index[:, None] == labels[None, :]).astype(jnp.float32)
    own_hot = lax.dynamic_slice_in_dim(all_hot, start, img_dev, 0)
    first_kernel, second_kernel, third_kernel = (
        lax.all_gather(first_atrous_weight, "dp", axis=2, tiled=True),
        lax.all_gather(second_atrous_weight, "dp", axis=2, tiled=True),
        lax.all_gather(third_atrous_weight, "dp", axis=2, tiled=True),
    )
    pointwise_output = jnp.einsum(
        "irwc,co->irwo", features, pointwise_weight, preferred_element_type=jnp.float32
    )
    pre = jnp.concatenate(
        [
            pointwise_output,
            dilated_result(features, first_kernel, DILATION_FIRST),
            dilated_result(features, second_kernel, DILATION_SECOND),
            dilated_result(features, third_kernel, DILATION_THIRD),
        ],
        -1,
    )
    group_first, group_second = stats_terms(pre, own_hot)
    pool_part = jnp.sum(features, axis=(1, 2), dtype=jnp.float32)
    pool_total = lax.psum(pool_part, "rows")
    total_first, total_second = lax.psum((group_first, group_second), ("dp", "rows"))
    branches = apply_norm(
        pre,
        own_hot,
        total_first,
        total_second,
        count,
        branch_norm_gain.reshape(-1),
        branch_norm_shift.reshape(-1),
    )
    pooled = (pool_total / pixels).astype(jnp.bfloat16)
    pool_act = jax.nn.relu(
        jnp.dot(pooled, pooling_weight, preferred_element_type=jnp.float32)
    ).astype(jnp.bfloat16)
    pool_map = jnp.broadcast_to(
        pool_act[:, None, None, :], (img_dev, rows_dev, cols, pool_act.shape[1])
    )
    joined = jnp.concatenate([branches, pool_map], -1)
    local_out = project(
        joined, own_hot, projection_weight, count, projection_norm_gain, projection_norm_shift
    )
    return lax.all_to_all(local_out, "dp", split_axis=2, concat_axis=0, tiled=True)


def solution(mesh):
    in_specs = (
        P("dp", "rows", None, None),
        P(None, None, "dp", None),
        P(None, None, "dp", None),
        P(None, None, "dp", None),
        P(),
        P(),
        P(),
        P(),
        P(),
        P(),
        P(),
        P(),
    )
    out_specs = P(None, "rows", "dp", None)
    return jax.shard_map(shards, mesh=mesh, in_specs=in_specs, out_specs=out_specs, check_vma=False)
```

profile of v0, /device:TPU:1, one launch (start us, length us, event | category | flops | bytes accessed | tf_op | source)
XLA Modules:
  0.0 726.8 jit_solution(7017526560821502395)
XLA Ops:
  6.5 0.7 all-gather.4.cloned.1.call-update
  7.3 0.7 all-gather.6.cloned.1.call-update
  8.1 0.7 all-gather.8.cloned.1.call-update
  8.8 1.3 collective-permute-start.1
  10.1 7.5 %collective-permute-start = (bf16[2,6,64,1024]{3,2,1,0:T(8,128)(2,1)}, bf16[2,6,64,1024]{3,2,1,0:T(8,128)(2,1)}, u32[]{:S(2)}, u32[]{:S(2)}) collective-permute-start(bf16[2,6,64,1024]{3,2,1,0:T(8,128)(2,1)} %param.12), channel_id=1, source_target_pairs={{0,2},{1,3},{2,4},{3,5},{4,6},{5,7},{8,10},{9,11},{10,12},{11,13},... | collective-permute-start | bytes 4718600 | tf_op jit(solution)/shard_map/ppermute | solution.py:14
  17.6 1.3 collective-permute-start.3
  18.9 11.2 %collective-permute-start.2 = (bf16[2,6,64,1024]{3,2,1,0:T(8,128)(2,1)}, bf16[2,6,64,1024]{3,2,1,0:T(8,128)(2,1)}, u32[]{:S(2)}, u32[]{:S(2)}) collective-permute-start(bf16[2,6,64,1024]{3,2,1,0:T(8,128)(2,1)} %param.12), channel_id=1, source_target_pairs={{0,4},{1,5},{2,6},{3,7},{8,12},{9,13},{10,14},{11,15},{16,20},{17,... | collective-permute-start | bytes 4718600 | tf_op jit(solution)/shard_map/ppermute | solution.py:14
  30.1 1.3 collective-permute-start.5
  31.4 0.7 dynamic-slice
  32.1 1.7 convert_reduce_fusion
  33.9 146.7 %psum.37 = f32[2,1024]{1,0:T(2,128)S(1)} all-reduce(f32[2,1024]{1,0:T(2,128)S(1)} %convert_reduce_fusion), channel_id=1, replica_groups=mesh['dp'=32,'rows'=8] {'rows'}, use_global_device_ids=true, to_apply=%region_5.6 | all-reduce | flops 2048 | bytes 16384 | tf_op jit(solution)/shard_map/psum | solution.py:115
  180.5 2.1 fusion.49
  182.7 2.4 collective-permute-start.4
  185.1 3.4 fusion.10
  188.5 1.4 slice_bitcast_fusion.36
  189.9 2.8 fusion.11
  192.7 1.4 slice_bitcast_fusion.39
  194.1 1.4 fusion.12
  195.5 1.3 slice_bitcast_fusion.42
  196.8 0.6 copy-done.17
  197.4 90.0 %all-gather.6.cloned.1.call-done = bf16[3,3,1024,256]{3,2,1,0:T(8,128)(2,1)} async-done(((bf16[3,3,32,256]{3,2,1,0:T(8,128)(2,1)}), bf16[3,3,1024,256]{3,2,1,0:T(8,128)(2,1)}) %all-gather.6.cloned.1.call-update) | async-done | bytes 4718608 | tf_op jit(solution)/shard_map/all_gather | solution.py:98
  287.4 3.4 fusion.7
  290.8 1.4 slice_bitcast_fusion.27
  292.3 2.8 fusion.8
  295.1 1.4 slice_bitcast_fusion.30
  296.5 1.4 fusion.9
  297.9 1.5 slice_bitcast_fusion.33
  299.3 0.5 copy-done.20
  299.8 61.1 %all-gather.8.cloned.1.call-done = bf16[3,3,1024,256]{3,2,1,0:T(8,128)(2,1)} async-done(((bf16[3,3,32,256]{3,2,1,0:T(8,128)(2,1)}), bf16[3,3,1024,256]{3,2,1,0:T(8,128)(2,1)}) %all-gather.8.cloned.1.call-update) | async-done | bytes 4718608 | tf_op jit(solution)/shard_map/all_gather | solution.py:99
  361.0 3.4 fusion.4
  364.5 2.8 fusion.5
  367.3 0.1 slice_bitcast_fusion.21
  367.5 1.4 fusion.6
  369.1 0.9 copy-done.3
  370.0 0.2 copy-done.4
  370.3 0.2 copy-done.5
  370.5 0.2 copy-done.6
  370.8 2.3 fusion.26
  373.1 0.2 copy-done.12
  373.3 0.2 copy-done.13
  373.5 0.2 copy-done.14
  373.8 1.9 fusion.34
  375.7 0.6 fusion.42
  376.3 0.9 copy-done.1
  377.2 0.4 fusion.48
  377.6 0.9 fusion.79
  378.5 0.9 fusion.78
  379.5 0.2 fusion.22
  379.6 0.7 copy.119
  380.3 0.7 copy.120
  381.0 237.9 %all-reduce.22.cloned.1.call-done = (f32[16,1024]{1,0:T(8,128)}, f32[16,1024]{1,0:T(8,128)}) async-done(((f32[16,1024]{1,0:T(8,128)}, f32[16,1024]{1,0:T(8,128)}), (f32[16,1024]{1,0:T(8,128)}, f32[16,1024]{1,0:T(8,128)})) %all-reduce.22.cloned.1.call-update) | async-done | bytes 131088 | tf_op jit(solution)/shard_map/psum | solution.py:116
  618.9 1.0 fusion.58
  620.0 1.1 fusion.51
  621.0 1.7 maximum_convert_fusion
  622.8 0.7 fusion.96
  623.6 0.3 fusion.77
  623.8 0.3 fusion.76
  624.1 76.6 %all-reduce.18 = (f32[16,256]{1,0:T(8,128)S(1)}, f32[16,256]{1,0:T(8,128)S(1)}) all-reduce(f32[16,256]{1,0:T(8,128)S(1)} %fusion.76, f32[16,256]{1,0:T(8,128)S(1)} %fusion.77), channel_id=1, replica_groups=mesh['dp'=32,'rows'=8] {'dp','rows'}, use_global_device_ids=true, to_apply=%region_9.10 | all-reduce | flops 8192 | bytes 65536 | tf_op jit(solution)/shard_map/psum | solution.py:65
  700.7 0.2 fusion.70
  700.9 0.2 fusion.63
  701.1 0.2 maximum_convert_fusion.1
  701.2 0.4 copy.97
  701.6 17.6 %all_to_all.18 = bf16[2,6,64,256]{3,0,1,2:T(2,128)(2,1)S(1)} all-to-all(bf16[2,6,64,256]{3,0,1,2:T(2,128)(2,1)S(1)} %copy.97), channel_id=1, replica_groups=mesh['dp'=32,'rows'=8] {'dp'}, dimensions={2} | all-to-all | bytes 786432 | tf_op jit(solution)/shard_map/all_to_all | solution.py:137
  719.3 1.0 copy.98
  (59 shorter events, 0.6 us)
Async XLA Ops:
  6.5 616.3 %copy-start = (bf16[1280,256]{1,0:T(8,128)(2,1)S(1)}, bf16[1280,256]{1,0:T(8,128)(2,1)}, u32[]{:S(2)}) copy-start(bf16[1280,256]{1,0:T(8,128)(2,1)} %param.18) | copy-start | bytes 1966084
  6.5 178.6 %all-gather.4.cloned.1.call-start = ((), (), s32[]{:S(2)}) async-start(), calls=%async_computation.1 | async-start | bytes 4866048 | tf_op jit(solution)/shard_map/all_gather | solution.py:97
  7.3 280.2 %all-gather.6.cloned.1.call-start = ((), (), s32[]{:S(2)}) async-start(), calls=%async_computation.2 | async-start | bytes 4866048 | tf_op jit(solution)/shard_map/all_gather | solution.py:98
  8.0 174.6 %copy-start.2 = (bf16[2,6,64,1024]{3,2,1,0:T(8,128)(2,1)S(1)}, bf16[2,6,64,1024]{3,2,1,0:T(8,128)(2,1)}, u32[]{:S(2)}) copy-start(bf16[2,6,64,1024]{3,2,1,0:T(8,128)(2,1)} %param.12) | copy-start | bytes 4718596
  8.0 352.9 %all-gather.8.cloned.1.call-start = ((), (), s32[]{:S(2)}) async-start(), calls=%async_computation.3 | async-start | bytes 4866048 | tf_op jit(solution)/shard_map/all_gather | solution.py:99
  8.8 610.2 %all-reduce.22.cloned.1.call-start = ((), (), s32[]{:S(2)}) async-start(), calls=%async_computation.4 | async-start | bytes 262144 | tf_op jit(solution)/shard_map/psum | solution.py:116
  8.8 173.8 %collective-permute-start.1 = (bf16[2,6,64,1024]{3,2,1,0:T(8,128)(2,1)}, bf16[2,6,64,1024]{3,2,1,0:T(8,128)(2,1)}, u32[]{:S(2)}, u32[]{:S(2)}) collective-permute-start(bf16[2,6,64,1024]{3,2,1,0:T(8,128)(2,1)} %param.12), channel_id=1, source_target_pairs={{2,0},{3,1},{4,2},{5,3},{6,4},{7,5},{10,8},{11,9},{12,10},{13,11},... | collective-permute-start | bytes 4718600 | tf_op jit(solution)/shard_map/ppermute | solution.py:14
  10.1 179.8 %collective-permute-start = (bf16[2,6,64,1024]{3,2,1,0:T(8,128)(2,1)}, bf16[2,6,64,1024]{3,2,1,0:T(8,128)(2,1)}, u32[]{:S(2)}, u32[]{:S(2)}) collective-permute-start(bf16[2,6,64,1024]{3,2,1,0:T(8,128)(2,1)} %param.12), channel_id=1, source_target_pairs={{0,2},{1,3},{2,4},{3,5},{4,6},{5,7},{8,10},{9,11},{10,12},{11,13},... | collective-permute-start | bytes 4718600 | tf_op jit(solution)/shard_map/ppermute | solution.py:14
  17.6 179.9 %collective-permute-start.3 = (bf16[2,6,64,1024]{3,2,1,0:T(8,128)(2,1)}, bf16[2,6,64,1024]{3,2,1,0:T(8,128)(2,1)}, u32[]{:S(2)}, u32[]{:S(2)}) collective-permute-start(bf16[2,6,64,1024]{3,2,1,0:T(8,128)(2,1)} %param.12), channel_id=1, source_target_pairs={{4,0},{5,1},{6,2},{7,3},{12,8},{13,9},{14,10},{15,11},{20,16},{21,... | collective-permute-start | bytes 4718600 | tf_op jit(solution)/shard_map/ppermute | solution.py:14
  18.9 273.4 %collective-permute-start.2 = (bf16[2,6,64,1024]{3,2,1,0:T(8,128)(2,1)}, bf16[2,6,64,1024]{3,2,1,0:T(8,128)(2,1)}, u32[]{:S(2)}, u32[]{:S(2)}) collective-permute-start(bf16[2,6,64,1024]{3,2,1,0:T(8,128)(2,1)} %param.12), channel_id=1, source_target_pairs={{0,4},{1,5},{2,6},{3,7},{8,12},{9,13},{10,14},{11,15},{16,20},{17,... | collective-permute-start | bytes 4718600 | tf_op jit(solution)/shard_map/ppermute | solution.py:14
  30.1 269.7 %collective-permute-start.5 = (bf16[2,6,64,1024]{3,2,1,0:T(8,128)(2,1)}, bf16[2,6,64,1024]{3,2,1,0:T(8,128)(2,1)}, u32[]{:S(2)}, u32[]{:S(2)}) collective-permute-start(bf16[2,6,64,1024]{3,2,1,0:T(8,128)(2,1)} %param.12), channel_id=1, source_target_pairs={{6,0},{7,1},{14,8},{15,9},{22,16},{23,17},{30,24},{31,25},{38,32},... | collective-permute-start | bytes 4718600 | tf_op jit(solution)/shard_map/ppermute | solution.py:14
  182.7 181.9 %collective-permute-start.4 = (bf16[2,6,64,1024]{3,2,1,0:T(8,128)(2,1)S(1)}, bf16[2,6,64,1024]{3,2,1,0:T(8,128)(2,1)}, u32[]{:S(2)}, u32[]{:S(2)}) collective-permute-start(bf16[2,6,64,1024]{3,2,1,0:T(8,128)(2,1)S(1)} %copy-done.2), channel_id=1, source_target_pairs={{0,6},{1,7},{8,14},{9,15},{16,22},{17,23},{24,30},{25,31},{32,38},... | collective-permute-start | bytes 4718600 | tf_op jit(solution)/shard_map/ppermute | solution.py:14
  185.1 4.8 copy-start.26
  188.5 4.2 copy-start.15
  192.7 2.8 copy-start.16
  195.5 2.0 copy-start.17
  287.4 4.8 copy-start.25
  290.8 4.2 copy-start.18
  295.1 2.8 copy-start.19
  297.9 2.0 copy-start.20
  361.0 3.6 copy-start.24
  367.5 1.6 copy-start.7
  367.5 1.6 copy-start.8
  368.9 1.1 copy-start.3
  368.9 1.4 copy-start.4
  368.9 1.6 copy-start.5
  368.9 1.8 copy-start.6
  370.8 2.3 copy-start.9
  370.8 2.3 copy-start.10
  370.8 2.3 copy-start.11
  370.8 2.5 copy-start.12
  370.8 2.8 copy-start.13
  370.8 3.0 copy-start.14
  376.3 0.9 copy-start.1
  377.2 2.2 copy-start.21
  622.8 78.2 %copy-start.22 = (f32[256]{0:T(256)S(1)}, f32[256]{0:T(256)}, u32[]{:S(2)}) copy-start(f32[256]{0:T(256)} %param.22) | copy-start | bytes 3076
  622.8 78.2 %copy-start.23 = (f32[256]{0:T(256)S(1)}, f32[256]{0:T(256)}, u32[]{:S(2)}) copy-start(f32[256]{0:T(256)} %param.21) | copy-start | bytes 3076
Sparse Core Ops, SparseCore 0:
  9.2 144.8 all-gather.3
  156.0 131.4 all-gather.5
  289.3 71.6 all-gather.7
  379.6 239.3 all-reduce.21
where the time goes:
time: 728 us; the launch traced here: 727 us
  waiting for transfers between devices  391 us (54%)
  blocking collectives  241 us (33%)
  matrix products  30.6 us (4%)
  starting transfers between devices  25.1 us (3%)
  local copies, waits for them, and re-layouts  16.8 us (2%)
  between operations  13.6 us (2%)
  other arithmetic  8.76 us (1%)
    psum x1, waiting for transfers between devices, shards(): lax.psum((group_first, group_second), ('dp', 'rows'))  238 us
    psum x1, blocking collectives, shards(): pool_total = lax.psum(pool_part, 'rows')  147 us
    all_gather x1, waiting for transfers between devices, shards(): lax.all_gather(second_atrous_weight, 'dp', axis=2, tiled=True)  90 us
    psum x1, blocking collectives, project(): lax.psum((group_first, group_second), ('dp', 'rows'))  76.6 us
    all_gather x1, waiting for transfers between devices, shards(): lax.all_gather(third_atrous_weight, 'dp', axis=2, tiled=True)  61.1 us
    ppermute x6, starting transfers between devices, from_behind(): return lax.ppermute(array, axis, pairs)  25 us
    dot_general x9, matrix products, row_tap_list(): jnp.einsum('irwc,kco->irwko', block_tensor, kernel_row_slice, preferred_e...  22.8 us
    all_to_all x1, blocking collectives, shards(): lax.all_to_all(local_out, 'dp', split_axis=2, concat_axis=0, tiled=True)  17.6 us
  transfers between devices with their start and end apart: 10, of which 3 were waited for; matrix products, arithmetic and copies ran while one was open for 5% of the time, Pallas kernels for 0%

commit v1 on v0

--- a/solution.py
+++ b/solution.py
@@ -112,7 +112,7 @@
     )
     group_first, group_second = stats_terms(pre, own_hot)
     pool_part = jnp.sum(features, axis=(1, 2), dtype=jnp.float32)
-    pool_total = lax.psum(pool_part, "rows")
+    pool_total = jnp.sum(lax.all_gather(pool_part, "rows"), axis=0)
     total_first, total_second = lax.psum((group_first, group_second), ("dp", "rows"))
     branches = apply_norm(
         pre,

time: 728 us -> 743 us (1.021)
  waiting for transfers between devices: 391 us -> 400 us
    all_gather x0 -> x1, blocking collectives: none -> 152 us  [shards(): pool_total = jnp.sum(lax.all_gather(pool_part, 'rows'), axis=0)]
    psum x1 -> x0, blocking collectives: 147 us -> none  [shards(): pool_total = lax.psum(pool_part, 'rows')]
  transfers between devices with their start and end apart: 10 -> 10, of which waited for: 3 -> 3; matrix products, arithmetic and copies ran while one was open for 5% -> 4% of each run, Pallas kernels for 0% -> 0%
where the time goes in v1:
time: 743 us; the launch traced here: 742 us
  waiting for transfers between devices  400 us (54%)
  blocking collectives  247 us (33%)
  matrix products  29 us (4%)
  starting transfers between devices  27 us (4%)
  local copies, waits for them, and re-layouts  16.8 us (2%)
  between operations  13.6 us (2%)
  other arithmetic  8.83 us (1%)
    psum x1, waiting for transfers between devices, shards(): lax.psum((group_first, group_second), ('dp', 'rows'))  238 us
    all_gather x1, blocking collectives, shards(): pool_total = jnp.sum(lax.all_gather(pool_part, 'rows'), axis=0)  152 us
    all_gather x1, waiting for transfers between devices, shards(): lax.all_gather(second_atrous_weight, 'dp', axis=2, tiled=True)  94.9 us
    psum x1, blocking collectives, project(): lax.psum((group_first, group_second), ('dp', 'rows'))  76.6 us
    all_gather x1, waiting for transfers between devices, shards(): lax.all_gather(third_atrous_weight, 'dp', axis=2, tiled=True)  65.3 us
    ppermute x6, starting transfers between devices, from_behind(): return lax.ppermute(array, axis, pairs)  26.8 us
    dot_general x9, matrix products, row_tap_list(): jnp.einsum('irwc,kco->irwko', block_tensor, kernel_row_slice, preferred_e...  22.7 us
    all_to_all x1, blocking collectives, shards(): lax.all_to_all(local_out, 'dp', split_axis=2, concat_axis=0, tiled=True)  17.6 us
  transfers between devices with their start and end apart: 10, of which 3 were waited for; matrix products, arithmetic and copies ran while one was open for 4% of the time, Pallas kernels for 0%

profile of v1, /device:TPU:1, one launch (start us, length us, event | category | flops | bytes accessed | tf_op | source)
XLA Modules:
  0.0 742.1 jit_solution(6463600554907869608)
XLA Ops:
  6.5 0.7 all-gather.6.cloned.1.call-update
  7.3 0.7 all-gather.8.cloned.1.call-update
  8.1 0.7 all-gather.10.cloned.1.call-update
  8.8 1.3 collective-permute-start.1
  10.1 7.5 %collective-permute-start = (bf16[2,6,64,1024]{3,2,1,0:T(8,128)(2,1)}, bf16[2,6,64,1024]{3,2,1,0:T(8,128)(2,1)}, u32[]{:S(2)}, u32[]{:S(2)}) collective-permute-start(bf16[2,6,64,1024]{3,2,1,0:T(8,128)(2,1)} %param.12), channel_id=1, source_target_pairs={{0,2},{1,3},{2,4},{3,5},{4,6},{5,7},{8,10},{9,11},{10,12},{11,13},... | collective-permute-start | bytes 4718600 | tf_op jit(solution)/shard_map/ppermute | solution.py:14
  17.6 1.3 collective-permute-start.3
  18.8 11.3 %collective-permute-start.2 = (bf16[2,6,64,1024]{3,2,1,0:T(8,128)(2,1)}, bf16[2,6,64,1024]{3,2,1,0:T(8,128)(2,1)}, u32[]{:S(2)}, u32[]{:S(2)}) collective-permute-start(bf16[2,6,64,1024]{3,2,1,0:T(8,128)(2,1)} %param.12), channel_id=1, source_target_pairs={{0,4},{1,5},{2,6},{3,7},{8,12},{9,13},{10,14},{11,15},{16,20},{17,... | collective-permute-start | bytes 4718600 | tf_op jit(solution)/shard_map/ppermute | solution.py:14
  30.1 1.3 collective-permute-start.5
  31.4 0.7 dynamic-slice
  32.2 1.7 convert_reduce_fusion
  33.9 152.4 %all-gather.1 = f32[8,2,1024]{2,1,0:T(2,128)S(1)} all-gather(f32[1,2,1024]{2,1,0:T(2,128)S(1)} %bitcast.188), channel_id=2, replica_groups=mesh['dp'=32,'rows'=8] {'rows'}, dimensions={0}, use_global_device_ids=true | all-gather | bytes 73728 | tf_op jit(solution)/shard_map/all_gather | solution.py:115
  186.4 0.6 fusion.49
  187.0 4.2 collective-permute-start.4
  191.2 3.4 fusion.10
  194.6 1.4 slice_bitcast_fusion.36
  196.0 2.8 fusion.11
  198.8 1.4 slice_bitcast_fusion.39
  200.2 1.4 fusion.12
  201.6 1.3 slice_bitcast_fusion.42
  202.9 0.6 copy-done.17
  203.5 94.9 %all-gather.8.cloned.1.call-done = bf16[3,3,1024,256]{3,2,1,0:T(8,128)(2,1)} async-done(((bf16[3,3,32,256]{3,2,1,0:T(8,128)(2,1)}), bf16[3,3,1024,256]{3,2,1,0:T(8,128)(2,1)}) %all-gather.8.cloned.1.call-update) | async-done | bytes 4718608 | tf_op jit(solution)/shard_map/all_gather | solution.py:98
  298.5 3.4 fusion.7
  301.9 1.4 slice_bitcast_fusion.27
  303.3 2.8 fusion.8
  306.2 1.4 slice_bitcast_fusion.30
  307.6 1.4 fusion.9
  309.0 1.5 slice_bitcast_fusion.33
  310.5 0.5 copy-done.20
  310.9 65.3 %all-gather.10.cloned.1.call-done = bf16[3,3,1024,256]{3,2,1,0:T(8,128)(2,1)} async-done(((bf16[3,3,32,256]{3,2,1,0:T(8,128)(2,1)}), bf16[3,3,1024,256]{3,2,1,0:T(8,128)(2,1)}) %all-gather.10.cloned.1.call-update) | async-done | bytes 4718608 | tf_op jit(solution)/shard_map/all_gather | solution.py:99
  376.3 3.4 fusion.4
  379.7 0.1 slice_bitcast_fusion.18
  379.9 2.8 fusion.5
  382.8 1.4 fusion.6
  384.4 0.9 copy-done.3
  385.3 0.2 copy-done.4
  385.6 0.2 copy-done.5
  385.8 0.2 copy-done.6
  386.1 2.3 fusion.26
  388.4 0.2 copy-done.12
  388.6 0.2 copy-done.13
  388.9 0.2 copy-done.14
  389.1 1.9 fusion.34
  391.0 0.6 fusion.42
  391.6 0.9 copy-done.1
  392.5 0.4 fusion.48
  392.9 0.9 fusion.79
  393.8 0.9 fusion.78
  394.8 0.2 fusion.22
  395.0 0.7 copy.119
  395.6 0.7 copy.120
  396.3 237.9 %all-reduce.22.cloned.1.call-done = (f32[16,1024]{1,0:T(8,128)}, f32[16,1024]{1,0:T(8,128)}) async-done(((f32[16,1024]{1,0:T(8,128)}, f32[16,1024]{1,0:T(8,128)}), (f32[16,1024]{1,0:T(8,128)}, f32[16,1024]{1,0:T(8,128)})) %all-reduce.22.cloned.1.call-update) | async-done | bytes 131088 | tf_op jit(solution)/shard_map/psum | solution.py:116
  634.2 1.0 fusion.58
  635.3 1.1 fusion.51
  636.4 1.7 maximum_convert_fusion
  638.2 0.7 fusion.96
  638.9 0.3 fusion.77
  639.1 0.3 fusion.76
  639.4 76.6 %all-reduce.18 = (f32[16,256]{1,0:T(8,128)S(1)}, f32[16,256]{1,0:T(8,128)S(1)}) all-reduce(f32[16,256]{1,0:T(8,128)S(1)} %fusion.76, f32[16,256]{1,0:T(8,128)S(1)} %fusion.77), channel_id=1, replica_groups=mesh['dp'=32,'rows'=8] {'dp','rows'}, use_global_device_ids=true, to_apply=%region_9.10 | all-reduce | flops 8192 | bytes 65536 | tf_op jit(solution)/shard_map/psum | solution.py:65
  716.0 0.2 fusion.70
  716.2 0.2 fusion.63
  716.4 0.2 maximum_convert_fusion.1
  716.5 0.4 copy.97
  716.9 17.6 %all_to_all.18 = bf16[2,6,64,256]{3,0,1,2:T(2,128)(2,1)S(1)} all-to-all(bf16[2,6,64,256]{3,0,1,2:T(2,128)(2,1)S(1)} %copy.97), channel_id=1, replica_groups=mesh['dp'=32,'rows'=8] {'dp'}, dimensions={2} | all-to-all | bytes 786432 | tf_op jit(solution)/shard_map/all_to_all | solution.py:137
  734.5 1.0 copy.98
  (62 shorter events, 0.6 us)
Async XLA Ops:
  6.5 631.6 %copy-start = (bf16[1280,256]{1,0:T(8,128)(2,1)S(1)}, bf16[1280,256]{1,0:T(8,128)(2,1)}, u32[]{:S(2)}) copy-start(bf16[1280,256]{1,0:T(8,128)(2,1)} %param.18) | copy-start | bytes 1966084
  6.5 179.8 %copy-start.2 = (bf16[2,6,64,1024]{3,2,1,0:T(8,128)(2,1)S(1)}, bf16[2,6,64,1024]{3,2,1,0:T(8,128)(2,1)}, u32[]{:S(2)}) copy-start(bf16[2,6,64,1024]{3,2,1,0:T(8,128)(2,1)} %param.12) | copy-start | bytes 4718596
  6.5 179.8 %copy-start.22 = (bf16[1024,256]{1,0:T(8,128)(2,1)S(1)}, bf16[1024,256]{1,0:T(8,128)(2,1)}, u32[]{:S(2)}) copy-start(bf16[1024,256]{1,0:T(8,128)(2,1)} %param.16) | copy-start | bytes 1572868
  6.5 184.7 %all-gather.6.cloned.1.call-start = ((), (), s32[]{:S(2)}) async-start(), calls=%async_computation.1 | async-start | bytes 4866048 | tf_op jit(solution)/shard_map/all_gather | solution.py:97
  7.3 291.2 %all-gather.8.cloned.1.call-start = ((), (), s32[]{:S(2)}) async-start(), calls=%async_computation.2 | async-start | bytes 4866048 | tf_op jit(solution)/shard_map/all_gather | solution.py:98
  8.0 368.3 %all-gather.10.cloned.1.call-start = ((), (), s32[]{:S(2)}) async-start(), calls=%async_computation.3 | async-start | bytes 4866048 | tf_op jit(solution)/shard_map/all_gather | solution.py:99
  8.7 625.5 %all-reduce.22.cloned.1.call-start = ((), (), s32[]{:S(2)}) async-start(), calls=%async_computation.4 | async-start | bytes 262144 | tf_op jit(solution)/shard_map/psum | solution.py:116
  8.8 178.2 %collective-permute-start.1 = (bf16[2,6,64,1024]{3,2,1,0:T(8,128)(2,1)}, bf16[2,6,64,1024]{3,2,1,0:T(8,128)(2,1)}, u32[]{:S(2)}, u32[]{:S(2)}) collective-permute-start(bf16[2,6,64,1024]{3,2,1,0:T(8,128)(2,1)} %param.12), channel_id=1, source_target_pairs={{2,0},{3,1},{4,2},{5,3},{6,4},{7,5},{10,8},{11,9},{12,10},{13,11},... | collective-permute-start | bytes 4718600 | tf_op jit(solution)/shard_map/ppermute | solution.py:14
  10.1 185.9 %collective-permute-start = (bf16[2,6,64,1024]{3,2,1,0:T(8,128)(2,1)}, bf16[2,6,64,1024]{3,2,1,0:T(8,128)(2,1)}, u32[]{:S(2)}, u32[]{:S(2)}) collective-permute-start(bf16[2,6,64,1024]{3,2,1,0:T(8,128)(2,1)} %param.12), channel_id=1, source_target_pairs={{0,2},{1,3},{2,4},{3,5},{4,6},{5,7},{8,10},{9,11},{10,12},{11,13},... | collective-permute-start | bytes 4718600 | tf_op jit(solution)/shard_map/ppermute | solution.py:14
  17.6 186.0 %collective-permute-start.3 = (bf16[2,6,64,1024]{3,2,1,0:T(8,128)(2,1)}, bf16[2,6,64,1024]{3,2,1,0:T(8,128)(2,1)}, u32[]{:S(2)}, u32[]{:S(2)}) collective-permute-start(bf16[2,6,64,1024]{3,2,1,0:T(8,128)(2,1)} %param.12), channel_id=1, source_target_pairs={{4,0},{5,1},{6,2},{7,3},{12,8},{13,9},{14,10},{15,11},{20,16},{21,... | collective-permute-start | bytes 4718600 | tf_op jit(solution)/shard_map/ppermute | solution.py:14
  18.8 284.5 %collective-permute-start.2 = (bf16[2,6,64,1024]{3,2,1,0:T(8,128)(2,1)}, bf16[2,6,64,1024]{3,2,1,0:T(8,128)(2,1)}, u32[]{:S(2)}, u32[]{:S(2)}) collective-permute-start(bf16[2,6,64,1024]{3,2,1,0:T(8,128)(2,1)} %param.12), channel_id=1, source_target_pairs={{0,4},{1,5},{2,6},{3,7},{8,12},{9,13},{10,14},{11,15},{16,20},{17,... | collective-permute-start | bytes 4718600 | tf_op jit(solution)/shard_map/ppermute | solution.py:14
  30.1 280.8 %collective-permute-start.5 = (bf16[2,6,64,1024]{3,2,1,0:T(8,128)(2,1)}, bf16[2,6,64,1024]{3,2,1,0:T(8,128)(2,1)}, u32[]{:S(2)}, u32[]{:S(2)}) collective-permute-start(bf16[2,6,64,1024]{3,2,1,0:T(8,128)(2,1)} %param.12), channel_id=1, source_target_pairs={{6,0},{7,1},{14,8},{15,9},{22,16},{23,17},{30,24},{31,25},{38,32},... | collective-permute-start | bytes 4718600 | tf_op jit(solution)/shard_map/ppermute | solution.py:14
  187.0 192.9 %collective-permute-start.4 = (bf16[2,6,64,1024]{3,2,1,0:T(8,128)(2,1)S(1)}, bf16[2,6,64,1024]{3,2,1,0:T(8,128)(2,1)}, u32[]{:S(2)}, u32[]{:S(2)}) collective-permute-start(bf16[2,6,64,1024]{3,2,1,0:T(8,128)(2,1)S(1)} %copy-done.2), channel_id=1, source_target_pairs={{0,6},{1,7},{8,14},{9,15},{16,22},{17,23},{24,30},{25,31},{32,38},... | collective-permute-start | bytes 4718600 | tf_op jit(solution)/shard_map/ppermute | solution.py:14
  191.2 4.8 copy-start.27
  194.6 4.2 copy-start.15
  198.8 2.8 copy-start.16
  201.6 2.0 copy-start.17
  298.5 4.9 copy-start.26
  301.9 4.2 copy-start.18
  306.1 2.8 copy-start.19
  309.0 2.0 copy-start.20
  376.3 3.6 copy-start.25
  382.8 1.6 copy-start.7
  382.8 1.6 copy-start.8
  384.2 1.1 copy-start.3
  384.2 1.4 copy-start.4
  384.2 1.6 copy-start.5
  384.2 1.8 copy-start.6
  386.1 2.3 copy-start.9
  386.1 2.3 copy-start.10
  386.1 2.4 copy-start.11
  386.1 2.5 copy-start.12
  386.1 2.8 copy-start.13
  386.1 3.0 copy-start.14
  391.6 0.9 copy-start.1
  392.5 2.2 copy-start.21
  638.1 78.2 %copy-start.23 = (f32[256]{0:T(256)S(1)}, f32[256]{0:T(256)}, u32[]{:S(2)}) copy-start(f32[256]{0:T(256)} %param.22) | copy-start | bytes 3076
  638.1 78.2 %copy-start.24 = (f32[256]{0:T(256)S(1)}, f32[256]{0:T(256)}, u32[]{:S(2)}) copy-start(f32[256]{0:T(256)} %param.21) | copy-start | bytes 3076
Sparse Core Ops, SparseCore 0:
  9.2 141.9 all-gather.5
  153.1 145.3 all-gather.7
  300.4 75.8 all-gather.9
  394.9 239.3 all-reduce.21
